TPU v7x, 256 devices: a whole 4x4x8 slice. The times are simulated.
256 devices in a mesh: dp: 32 (over x, z), expert: 8 (over y, core).
Axes of the slice: x: 4, y: 4, z: 8, core: 2. Of those that a mesh axis runs over, the one named last changes fastest.
Arguments:
- tokens: bfloat16 [32768, 2048], P(('dp', 'expert')), may hold values from -6 to 6
- cotangent: bfloat16 [32768, 2048], P(('dp', 'expert')), may hold values from -6 to 6
- down_vectors: bfloat16 [120, 64, 2048], P('expert'), may hold values from -0.125 to 0.125
- up_vectors: bfloat16 [120, 64, 2048], P('expert'), may hold values from -0.1875 to 0.1875
- block_ids: int32 [256, 16], P(('dp', 'expert')), may hold values from 0 to 119, as said below
Outputs:
- output: bfloat16 [32768, 2048], P(('dp', 'expert'))
- input_grad: bfloat16 [32768, 2048], P(('dp', 'expert'))
- down_grad: float32 [120, 64, 2048], P('expert', None, 'dp')
- up_grad: float32 [120, 64, 2048], P('expert', None, 'dp')
Inputs may be any that keep to these rules, and one draw needn't show every extreme that they name: `block_ids`: the 16 ids of one tile are distinct. At most 4 of them lie in one slab (ids s * 15 to (s + 1) * 15 - 1), and every tile has exactly 4 in some slab.
All inputs are finite; a program needn't handle non-finite values.
Results may differ from a plain program's by a relative error of at most 0.02.
Values may be sent and summed in bfloat16 or wider, within the bound.
A program may use at most 192 MiB of HBM per device.

v0:
```python
import jax
import jax.numpy as jnp
from jax import lax
from jax.sharding import PartitionSpec as P


def silu_slope(argument):
    sigmoid_val = jax.nn.sigmoid(argument)
    return sigmoid_val * (1.0 + argument * (1.0 - sigmoid_val))


def slot_table(block_ids, slab_count, most_slots, per_slab):
    owner_slab = block_ids // per_slab
    local_block = block_ids % per_slab
    member = (
        owner_slab[:, :, None] == jnp.arange(slab_count, dtype=jnp.int32)[None, None, :]
    ).astype(jnp.int32)
    run_order = jnp.cumsum(member, axis=1) - 1
    rank_in = jnp.sum(run_order * member, axis=2)
    slot_hit = member[:, :, :, None] * (
        rank_in[:, :, None, None] == jnp.arange(most_slots, dtype=jnp.int32)[None, None, None, :]
    ).astype(jnp.int32)
    filled = jnp.sum(slot_hit, axis=1)
    chosen = jnp.sum(slot_hit * local_block[:, :, None, None], axis=1)
    return chosen + filled - 1


def body(tokens, cotangent, down_vectors, up_vectors, block_ids):
    slab_count = lax.axis_size("expert")
    per_slab = down_vectors.shape[0]
    width = tokens.shape[1]
    tile_count = block_ids.shape[0]
    tile_rows = tokens.shape[0] // tile_count
    most_slots = 2 * block_ids.shape[1] // slab_count
    slot_ids = slot_table(block_ids, slab_count, most_slots, per_slab).astype(jnp.bfloat16)
    tok_tiles = tokens.reshape(tile_count, tile_rows, width)
    cot_tiles = cotangent.reshape(tile_count, tile_rows, width)
    all_tok, all_cot, all_slots = (
        lax.all_gather(tok_tiles, "expert", axis=0, tiled=True),
        lax.all_gather(cot_tiles, "expert", axis=0, tiled=True),
        lax.all_gather(slot_ids, "expert", axis=0, tiled=True),
    )
    own_slab = lax.axis_index("expert")
    own_slots = lax.dynamic_index_in_dim(all_slots, own_slab, axis=1, keepdims=False).astype(
        jnp.int32
    )
    live_slot = own_slots >= 0
    safe_index = jnp.maximum(own_slots, 0)
    live_mask = live_slot.astype(jnp.float32)[:, None, :, None]
    down_sel = jnp.take(down_vectors, safe_index, axis=0)
    up_sel = jnp.take(up_vectors, safe_index, axis=0)
    scores = jnp.einsum("gtd,gsed->gtse", all_tok, down_sel, preferred_element_type=jnp.float32)
    hidden = (jax.nn.silu(scores) * live_mask).astype(jnp.bfloat16)
    output_part = jnp.einsum("gtse,gsed->gtd", hidden, up_sel, preferred_element_type=jnp.float32)
    output_sum = lax.psum_scatter(
        output_part.astype(jnp.bfloat16), "expert", scatter_dimension=0, tiled=True
    ).astype(jnp.float32)
    back_hidden = jnp.einsum("gtd,gsed->gtse", all_cot, up_sel, preferred_element_type=jnp.float32)
    back_scores = (back_hidden * silu_slope(scores) * live_mask).astype(jnp.bfloat16)
    input_part = jnp.einsum(
        "gtse,gsed->gtd", back_scores, down_sel, preferred_element_type=jnp.float32
    )
    input_sum = lax.psum_scatter(
        input_part.astype(jnp.bfloat16), "expert", scatter_dimension=0, tiled=True
    ).astype(jnp.float32)
    output = output_sum.reshape(tile_count * tile_rows, width).astype(jnp.bfloat16)
    input_grad = input_sum.reshape(tile_count * tile_rows, width).astype(jnp.bfloat16)
    expert_count = down_vectors.shape[1]
    down_terms = jnp.einsum(
        "gtse,gtd->gsed", back_scores, all_tok, preferred_element_type=jnp.float32
    )
    up_terms = jnp.einsum("gtse,gtd->gsed", hidden, all_cot, preferred_element_type=jnp.float32)
    flat_slots = safe_index.reshape(-1)
    empty_grads = jnp.zeros(down_vectors.shape, jnp.float32)
    down_slab = empty_grads.at[flat_slots].add(down_terms.reshape(-1, expert_count, width))
    up_slab = empty_grads.at[flat_slots].add(up_terms.reshape(-1, expert_count, width))
    down_grad, up_grad = (
        lax.psum_scatter(
            down_slab.astype(jnp.bfloat16), "dp", scatter_dimension=2, tiled=True
        ).astype(jnp.float32),
        lax.psum_scatter(
            up_slab.astype(jnp.bfloat16), "dp", scatter_dimension=2, tiled=True
        ).astype(jnp.float32),
    )
    return (output, input_grad, down_grad, up_grad)


def solution(mesh):
    placed = (
        P(("dp", "expert"), None),
        P(("dp", "expert"), None),
        P("expert", None, None),
        P("expert", None, None),
        P(("dp", "expert"), None),
    )
    return jax.shard_map(
        body,
        mesh=mesh,
        in_specs=placed,
        out_specs=(
            P(("dp", "expert"), None),
            P(("dp", "expert"), None),
            P("expert", None, "dp"),
            P("expert", None, "dp"),
        ),
        check_vma=False,
    )
```

profile of v0, /device:TPU:6, one launch (start us, length us, event | category | flops | bytes accessed | tf_op | source)
XLA Modules:
  0.0 702.2 jit_solution(17177514556547804258)
XLA Ops:
  9.9 10.8 %all-gather.3 = bf16[8,8,4]{1,2,0:T(4,128)(2,1)S(1)} all-gather(bf16[1,8,4]{1,2,0:T(4,128)(2,1)S(1)} %fusion.17), channel_id=2, replica_groups=mesh['dp'=32,'expert'=8] {'expert'}, dimensions={0}, use_global_device_ids=true | all-gather | bytes 576 | tf_op jit(solution)/shard_map/all_gather | solution.py:41
  21.2 7.1 %gather_fusion.1 = bf16[32,64,2048]{2,1,0:T(8,128)(2,1)} fusion(bf16[15,64,2048]{2,1,0:T(8,128)(2,1)} %param.10, s32[1024]{0:T(1024)S(1)} %pad_clamp_fusion), kind=kCustom, calls=%fused_computation.1.clone | custom fusion | bytes 16777344 | tf_op jit(solution)/shard_map/jit(_take)/gather | solution.py:51
  28.3 7.1 %gather_fusion = bf16[32,64,2048]{2,1,0:T(8,128)(2,1)} fusion(bf16[15,64,2048]{2,1,0:T(8,128)(2,1)} %param.9, s32[1024]{0:T(1024)S(1)} %pad_clamp_fusion), kind=kCustom, calls=%fused_computation.clone | custom fusion | bytes 16777344 | tf_op jit(solution)/shard_map/jit(_take)/gather | solution.py:50
  35.7 11.8 %all-gather.7.cloned.1.call-done = bf16[1024,2048]{1,0:T(8,128)(2,1)} async-done(((bf16[128,2048]{1,0:T(8,128)(2,1)}), bf16[1024,2048]{1,0:T(8,128)(2,1)}) %all-gather.7.cloned.1.call-update) | async-done | bytes 4194320 | tf_op jit(solution)/shard_map/all_gather | solution.py:39
  47.5 6.9 fusion.9
  54.4 29.6 %all-gather.9.cloned.1.call-done = bf16[1024,2048]{1,0:T(8,128)(2,1)} async-done(((bf16[128,2048]{1,0:T(8,128)(2,1)}), bf16[1024,2048]{1,0:T(8,128)(2,1)}) %all-gather.9.cloned.1.call-update) | async-done | bytes 4194320 | tf_op jit(solution)/shard_map/all_gather | solution.py:40
  84.0 7.1 %fusion.12 = bf16[8,128,4,64]{1,3,2,0:T(8,128)(2,1)S(1)} fusion(bf16[8,128,2048,1]{2,1,3,0:T(8,128)(2,1)} %bitcast.64, bf16[8,4,64,2048]{3,2,1,0:T(8,128)(2,1)} %bitcast.62, pred[8,4]{1,0:T(8,128)(4,1)S(1)} %copy.38, f32[8,128,4,64]{1,3,2,0:T(8,128)S(1)} %fusion.9, f32[8,4]{1,0:T(8,128)S(1)} %copy.40), kind=kOutput, calls=%fused_computation.20 | convolution fusion | flops 1080557568 | bytes 14155936 | tf_op jit(solution)/shard_map/gtd,gsed->gtse/dot_general | solution.py:58
  91.2 8.1 %fusion.25 = f32[8,4,64,2048]{3,2,1,0:T(8,128)} fusion(bf16[8,128,4,64]{1,3,2,0:T(8,128)(2,1)S(1)} %fusion.12, bf16[8,128,2048,1]{2,1,3,0:T(8,128)(2,1)S(1)} %bitcast.67), kind=kOutput, calls=%fused_computation.51 | convolution fusion | flops 1073741824 | bytes 21495808 | tf_op jit(solution)/shard_map/gtse,gtd->gsed/dot_general | solution.py:69
  99.3 4.0 broadcast_in_dim.8.clone
  103.3 34.1 %scatter_fusion = f32[15,64,2048]{2,1,0:T(8,128)} fusion(f32[15,64,2048]{2,1,0:T(8,128)} %broadcast_in_dim.8.clone, s32[32]{0:T(128)S(1)} %reshape.254, f32[32,64,2048]{2,1,0:T(8,128)} %bitcast.57), kind=kCustom, calls=%fused_computation.2 | custom fusion | flops 4194304 | bytes 50331776 | tf_op jit(solution)/shard_map/scatter-add | solution.py:75
  137.4 5.7 convert_element_type.114
  143.1 10.8 %copy.48 = bf16[15,64,2048]{1,0,2:T(8,128)(2,1)} copy(bf16[15,64,2048]{2,1,0:T(8,128)(2,1)} %convert_element_type.114) | data formatting | bytes 7864320
  153.9 11.8 %reshape.293 = bf16[2048,960]{1,0:T(8,128)(2,1)} reshape(bf16[2048,15,64]{2,1,0:T(8,128)(2,1)} %bitcast.58) | data formatting | bytes 7864320
  166.0 10.3 %fusion.24 = f32[8,4,64,2048]{3,2,1,0:T(8,128)} fusion(bf16[8,128,2048,1]{2,1,3,0:T(8,128)(2,1)} %bitcast.65, f32[8,128,4,64]{1,3,2,0:T(8,128)S(1)} %fusion.9, f32[8,4]{1,0:T(8,128)S(1)} %copy.40), kind=kOutput, calls=%fused_computation.50 | convolution fusion | flops 1075314688 | bytes 22020224 | tf_op jit(solution)/shard_map/gtse,gtd->gsed/dot_general | solution.py:72
  180.3 34.2 %scatter_fusion.1 = f32[15,64,2048]{2,1,0:T(8,128)} fusion(f32[15,64,2048]{2,1,0:T(8,128)} %broadcast_in_dim.8.clone.1, s32[32]{0:T(128)S(1)} %reshape.254, f32[32,64,2048]{2,1,0:T(8,128)} %bitcast.56), kind=kCustom, calls=%fused_computation.3 | custom fusion | flops 4194304 | bytes 50331776 | tf_op jit(solution)/shard_map/scatter-add | solution.py:76
  214.5 5.8 convert_element_type.116
  220.3 10.8 %copy.50 = bf16[15,64,2048]{1,0,2:T(8,128)(2,1)} copy(bf16[15,64,2048]{2,1,0:T(8,128)(2,1)} %convert_element_type.116) | data formatting | bytes 7864320
  231.1 11.8 %reshape.295 = bf16[2048,960]{1,0:T(8,128)(2,1)} reshape(bf16[2048,15,64]{2,1,0:T(8,128)(2,1)} %bitcast.59) | data formatting | bytes 7864320
  243.1 6.9 bitcast_convert_fusion.1
  250.0 6.8 bitcast_convert_fusion
  256.8 129.9 %reduce-scatter.13.cloned.1.call-done = bf16[64,960]{1,0:T(8,128)(2,1)} async-done(((bf16[2048,960]{1,0:T(8,128)(2,1)}), bf16[64,960]{1,0:T(8,128)(2,1)}) %reduce-scatter.13.cloned.1.call-update) | async-done | bytes 122896
  388.9 221.6 %reduce-scatter.15.cloned.1.call-done = bf16[64,960]{1,0:T(8,128)(2,1)} async-done(((bf16[2048,960]{1,0:T(8,128)(2,1)}), bf16[64,960]{1,0:T(8,128)(2,1)}) %reduce-scatter.15.cloned.1.call-update) | async-done | bytes 122896
  612.8 40.3 %reduce-scatter.9.cloned.1.call-done = bf16[1,128,2048]{2,1,0:T(8,128)(2,1)} async-done(((bf16[8,128,2048]{2,1,0:T(8,128)(2,1)}), bf16[1,128,2048]{2,1,0:T(8,128)(2,1)}) %reduce-scatter.9.cloned.1.call-update) | async-done | bytes 524304 | tf_op jit(solution)/shard_map/reduce_scatter | solution.py:55
  653.1 42.3 %reduce-scatter.11.cloned.1.call-done = bf16[1,128,2048]{2,1,0:T(8,128)(2,1)} async-done(((bf16[8,128,2048]{2,1,0:T(8,128)(2,1)}), bf16[1,128,2048]{2,1,0:T(8,128)(2,1)}) %reduce-scatter.11.cloned.1.call-update) | async-done | bytes 524304 | tf_op jit(solution)/shard_map/reduce_scatter | solution.py:63
  (42 shorter events, 12.3 us)
Async XLA Ops:
  7.2 40.3 %all-gather.7.cloned.1.call-start = ((), (), s32[]{:S(2)}) async-start(), calls=%async_computation.6 | async-start | bytes 4718592 | tf_op jit(solution)/shard_map/all_gather | solution.py:39
  7.9 76.1 %all-gather.9.cloned.1.call-start = ((), (), s32[]{:S(2)}) async-start(), calls=%async_computation.7 | async-start | bytes 4718592 | tf_op jit(solution)/shard_map/all_gather | solution.py:40
  8.6 378.1 %reduce-scatter.13.cloned.1.call-start = ((), (), s32[]{:S(2)}) async-start(), calls=%async_computation.8 | async-start | bytes 4325376
  84.0 7.2 %copy-start = (bf16[1024,2048]{1,0:T(8,128)(2,1)S(1)}, bf16[1024,2048]{1,0:T(8,128)(2,1)}, u32[]{:S(2)}) copy-start(bf16[1024,2048]{1,0:T(8,128)(2,1)} %all-gather.7.cloned.1.call-done) | copy-start | bytes 12582916
  165.8 444.8 %reduce-scatter.15.cloned.1.call-start = ((), (), s32[]{:S(2)}) async-start(), calls=%async_computation.9 | async-start | bytes 4325376
  243.0 410.1 %reduce-scatter.9.cloned.1.call-start = ((), (), s32[]{:S(2)}) async-start(), calls=%async_computation.4 | async-start | bytes 4718592 | tf_op jit(solution)/shard_map/reduce_scatter | solution.py:55
  250.0 445.4 %reduce-scatter.11.cloned.1.call-start = ((), (), s32[]{:S(2)}) async-start(), calls=%async_computation.5 | async-start | bytes 4718592 | tf_op jit(solution)/shard_map/reduce_scatter | solution.py:63
Sparse Core Ops, SparseCore 0:
  9.9 37.5 all-gather.6
  49.3 34.6 all-gather.8
  165.9 220.7 reduce-scatter.12
  391.0 219.5 reduce-scatter.14
  613.5 39.5 reduce-scatter.8
  656.1 39.2 reduce-scatter.10
where the time goes:
time: 704 us; the launch traced here: 702 us
  waiting for transfers between devices  477 us (68%)
  other arithmetic  82.7 us (12%)
  local copies, waits for them, and re-layouts  71.1 us (10%)
  matrix products  46.1 us (7%)
  between operations  14.2 us (2%)
  blocking collectives  10.8 us (2%)
    unnamed x8, waiting for transfers between devices  353 us
    unnamed x11, local copies, waits for them, and re-layouts  48.2 us
    reduce_scatter x1, waiting for transfers between devices, body(): lax.psum_scatter(input_part.astype(jnp.bfloat16), 'expert', scatter_dimen...  42.3 us
    reduce_scatter x1, waiting for transfers between devices, body(): lax.psum_scatter(output_part.astype(jnp.bfloat16), 'expert', scatter_dime...  40.3 us
    scatter-add x1, other arithmetic, body(): empty_grads.at[flat_slots].add(up_terms.reshape(-1, expert_count, width))  34.2 us
    scatter-add x1, other arithmetic, body(): empty_grads.at[flat_slots].add(down_terms.reshape(-1, expert_count, width))  34.1 us
    all_gather x1, waiting for transfers between devices, body(): lax.all_gather(cot_tiles, 'expert', axis=0, tiled=True)  29.6 us
  transfers between devices with their start and end apart: 6, of which 6 were waited for; matrix products, arithmetic and copies ran while one was open for 17% of the time, Pallas kernels for 0%

commit v1 on v0

v1 whole, which is shorter than its diff:
```python
import functools

import jax
import jax.numpy as jnp
from jax import lax
from jax.experimental import pallas as pl
from jax.experimental.pallas import tpu as pltpu
from jax.sharding import PartitionSpec as P

MESH = pl.DeviceIdType.MESH
BF16 = jnp.bfloat16
F32 = jnp.float32
ROWS_PAD = 1024
ZSIZE = 8
SLICE = 480
TOP, BOTTOM = pl.ds(0, 64), pl.ds(64, 64)
DOWN = (("x", 0, 2), ("x", 2, 4), ("x", 4, 6), ("x", 6, 8))
RATE, RATE_SIB, DELAY, DELAY_SIB = 44.5, 350.0, 2.0, 1.0


def rows_in(lo, hi):
    return pl.ds(lo * 64, min(hi * 64, SLICE) - lo * 64)


def kernel(xs, zs, *refs):
    ids, tok, cot, dn, up, out_o, in_o, dg_o, ug_o = refs[:9]
    dnv, upv, A, O, T, HB, pres, sibR, R1, R2, G, Rz, Rx = refs[9:22]
    rest = refs[22:]
    down_recv = [rest[2 * i : 2 * i + 2] for i in range(len(DOWN))]
    ssem, rsem, lsem = rest[2 * len(DOWN) :]
    width = tok.shape[1]
    slab_rows = dn.shape[0]
    quarter = width // xs
    row_step = quarter

    dp, e = lax.axis_index("dp"), lax.axis_index("expert")
    x, z = dp // zs, dp % zs
    y, k = e // 2, e % 2
    target = {
        "yp": (dp, ((y + 1) % 4) * 2 + k),
        "ym": (dp, ((y + 3) % 4) * 2 + k),
        "sib": (dp, y * 2 + (1 - k)),
        "xp": (((x + 1) % xs) * zs + z, e),
        "xm": (((x + xs - 1) % xs) * zs + z, e),
        "zp": (x * zs + (z + 1) % zs, e),
        "zm": (x * zs + (z + zs - 1) % zs, e),
    }
    spot = {"x": (x, xs), "z": (z, zs)}

    clock = [0.0]
    link_free = dict.fromkeys(target, 0.0)
    copies, landed, left, got, gone, events = [], [], [], set(), set(), {}
    steps = []

    def send(src, dst, to):
        i = len(copies)
        c = pltpu.make_async_remote_copy(
            src_ref=src, dst_ref=dst, send_sem=ssem.at[i], recv_sem=rsem.at[i],
            device_id=target[to], device_id_type=MESH,
        )
        c.start()
        kb = 1.0
        for d in src.shape:
            kb *= d
        kb *= jnp.dtype(src.dtype).itemsize / 1000
        begin = max(clock[0], link_free[to])
        link_free[to] = begin + kb / (RATE_SIB if to == "sib" else RATE)
        copies.append(c)
        left.append(link_free[to])
        landed.append(link_free[to] + (DELAY_SIB if to == "sib" else DELAY))
        return i

    def spend(us):
        clock[0] += us

    def mark(*name):
        events[name] = clock[0]

    def when(token):
        if isinstance(token, int):
            return landed[token]
        if token[0] == "sent":
            return left[token[1]]
        return events.get(token, float("inf"))

    def wait(token):
        if isinstance(token, int):
            if token not in got:
                got.add(token)
                copies[token].wait_recv()
        elif token[0] == "sent" and token[1] not in gone:
            gone.add(token[1])
            copies[token[1]].wait_send()

    def add(rank, step):
        steps.append([rank, step, next(step)])

    def run():
        while steps:
            ready = [max([when(t) for t in s[2]], default=0.0) for s in steps]
            now = [i for i in range(len(steps)) if ready[i] <= clock[0]]
            if now:
                i = min(now, key=lambda i: (steps[i][0], ready[i]))
            else:
                i = min(range(len(steps)), key=lambda i: ready[i])
                clock[0] = ready[i]
            assert ready[i] < float("inf")
            for t in steps[i][2]:
                wait(t)
            try:
                steps[i][2] = next(steps[i][1])
            except StopIteration:
                del steps[i]

    loads = []
    for i, (src, dst) in enumerate(
        (
            (tok, A.at[0, 0, 0]),
            (dn, dnv.at[pl.ds(0, slab_rows)]),
            (cot, A.at[1, 0, 0]),
            (up, upv.at[pl.ds(0, slab_rows)]),
        )
    ):
        loads.append(pltpu.make_async_copy(src, dst, lsem.at[i]))
        loads[-1].start()
    barrier = pltpu.get_barrier_semaphore()
    for dev in target.values():
        pl.semaphore_signal(barrier, inc=1, device_id=dev, device_id_type=MESH)

    lane = lax.broadcasted_iota(jnp.int32, (8, 128), 1)
    has = jnp.zeros((8, 128), F32)
    for j in range(ids.shape[1]):
        has = has + jnp.where(lane == ids[0, j], 1.0, 0.0)
    pres[0, 0] = has
    pl.semaphore_wait(barrier, len(target))

    half = {3: TOP, 1: BOTTOM}
    other = {3: BOTTOM, 1: TOP}
    ahead = {3: "yp", 1: "ym"}
    pres_sib = send(pres.at[0, 0], pres.at[0, 1], "sib")
    pres_near = {r: send(pres.at[0, 0], pres.at[r, 0], ahead[r]) for r in (3, 1)}
    near = {}
    for r in (3, 1):
        near[r, 0] = send(tok.at[half[r]], A.at[0, r, 0, half[r]], ahead[r])
    tok_sib = send(tok, A.at[0, 0, 1], "sib")
    for r in (3, 1):
        near[r, 1] = send(tok.at[other[r]], A.at[0, r, 0, other[r]], ahead[r])
    cot_sib = send(cot, A.at[1, 0, 1], "sib")
    for w in (dnv, upv):
        w[pl.ds(slab_rows, ROWS_PAD - slab_rows)] = jnp.zeros((ROWS_PAD - slab_rows, width), BF16)

    far, cots, on = {}, {}, {}

    def quarter_of(q):
        return pl.ds(q * quarter, quarter)

    def send_cot(r, q):
        for h in (half[r], other[r]):
            cots[r, q, h is other[r]] = send(
                cot.at[h, quarter_of(q)], A.at[1, r, 0, h, quarter_of(q)], ahead[r]
            )
        mark("cot out", r, q)

    def pass_presence(r):
        yield [pres_near[r]]
        if r == 3:
            far["pres"] = send(pres.at[3, 0], pres.at[2, 0], "yp")
            mark("far pres")
        on["pres", r] = send(pres.at[r, 0], pres.at[r, 1], "sib")
        mark("pres", r)

    def pass_far_presence():
        yield [("far pres",)]
        yield [far["pres"]]
        on["pres", 2] = send(pres.at[2, 0], pres.at[2, 1], "sib")
        mark("pres", 2)

    def pass_tokens(r):
        yield [near[r, 0]]
        far[r] = send(A.at[0, r, 0, half[r]], A.at[0, 2, 0, half[r]], ahead[r])
        mark("far", r)
        on[0, r, 0] = send(A.at[0, r, 0, half[r]], A.at[0, r, 1, half[r]], "sib")
        send_cot(r, 0)
        if xs > 1:
            send_cot(r, 1)
        yield [near[r, 1]]
        on[0, r, 1] = send(A.at[0, r, 0, other[r]], A.at[0, r, 1, other[r]], "sib")
        mark("tok", r)

    def pass_far_tokens():
        yield [("far", 3), ("far", 1)]
        for r in (3, 1):
            yield [far[r]]
            on[0, 2, r] = send(A.at[0, 2, 0, half[r]], A.at[0, 2, 1, half[r]], "sib")
        mark("tok", 2)

    def pass_cot(r):
        for q in range(xs):
            yield [("cot out", r, q)]
            yield [cots[r, q, False]]
            far[r, q] = send(
                A.at[1, r, 0, half[r], quarter_of(q)], A.at[1, 2, 0, half[r], quarter_of(q)], ahead[r]
            )
            mark("far cot", r, q)
            if q + 2 < xs:
                send_cot(r, q + 2)
            yield [cots[r, q, True]]
            on[1, r, q] = send(
                A.at[1, r, 0, :, quarter_of(q)], A.at[1, r, 1, :, quarter_of(q)], "sib"
            )
            mark("cot", r, q)

    def pass_far_cot():
        for q in range(xs):
            yield [("far cot", 3, q), ("far cot", 1, q)]
            yield [far[3, q], far[1, q]]
            on[1, 2, q] = send(
                A.at[1, 2, 0, :, quarter_of(q)], A.at[1, 2, 1, :, quarter_of(q)], "sib"
            )
            mark("cot", 2, q)

    def rows_of(r):
        return pl.ds(r * 256, 256)

    nt = (((1,), (1,)), ((), ()))

    def scores(r):
        def columns(n, carry):
            cols = pl.ds(pl.multiple_of(n * 256, 256), 256)
            s = lax.dot_general(
                A[0, r].reshape(256, width), dnv[cols, :], nt, preferred_element_type=F32
            )
            block = lax.broadcasted_iota(jnp.int32, (128, 256), 0) - e * 15
            column = lax.broadcasted_iota(jnp.int32, (128, 256), 1) + n * 256
            within = (column >= block * 64) & (column < block * 64 + 64)
            spread = jnp.where(within & (column < slab_rows), 1.0, 0.0).astype(BF16)
            live = [
                jnp.broadcast_to(
                    jnp.dot(pres[r, j].astype(BF16), spread, preferred_element_type=F32)[0:1],
                    (128, 256),
                )
                for j in range(2)
            ]
            live = jnp.concatenate(live, axis=0) > 0.5
            sig = 1.0 / (1.0 + jnp.exp(-s))
            slope = sig * (1.0 + s * (1.0 - sig))
            HB[0, rows_of(r), cols] = jnp.where(live, s * sig, 0.0).astype(BF16)
            HB[1, rows_of(r), cols] = jnp.where(live, slope, 0.0).astype(BF16)
            return carry

        lax.fori_loop(0, ROWS_PAD // 256, columns, 0)
        spend(1.8)

    def back(r):
        def columns(n, carry):
            cols = pl.ds(pl.multiple_of(n * 256, 256), 256)
            b = lax.dot_general(
                A[1, r].reshape(256, width), upv[cols, :], nt, preferred_element_type=F32
            )
            HB[1, rows_of(r), cols] = (b * HB[1, rows_of(r), cols].astype(F32)).astype(BF16)
            return carry

        lax.fori_loop(0, ROWS_PAD // 256, columns, 0)
        spend(1.6)

    def turn(a, r, lo, hi):
        def columns(d, carry):
            cols = pl.ds(pl.multiple_of(d * 128, 128), 128)
            T[a, cols, rows_of(r)] = A[a, r, :, :, cols].reshape(256, 128).T
            return carry

        lax.fori_loop(lo // 128, hi // 128, columns, 0)
        spend(0.6 * (hi - lo) / width)

    def parts_of(a, r):
        return O.at[a, r // 2] if r in (3, 1) else A.at[a, r]

    def partial(a, r):
        w = (upv, dnv)[a]
        to = parts_of(a, r)

        def columns(d, carry):
            cols = pl.ds(pl.multiple_of(d * 256, 256), 256)
            v = jnp.dot(HB[a, rows_of(r), :], w[:, cols], preferred_element_type=F32)
            to[:, :, cols] = v.astype(BF16).reshape(2, 128, 256)
            return carry

        lax.fori_loop(0, width // 256, columns, 0)
        spend(1.9)

    def gradient(table, q, pair):
        d = pl.ds(pl.multiple_of(q * row_step, row_step), row_step)
        c = pl.ds(pl.multiple_of(pair * 256, 256), 256)
        v = jnp.dot(T[table, d, :], HB[1 - table, :, c], preferred_element_type=F32)
        for j in range(2):
            w = v[:, j * 128 : (j + 1) * 128]
            w = w.reshape(zs, 64, 128)
            if j == 1 and isinstance(pair, int) and pair == 3:
                low = w[:, 32:64].reshape(zs * 32, 128)
                w = w[:, 0:32] + pltpu.roll(low, 64, 1).reshape(zs, 32, 128)
                G[table, q, :, pl.ds(448, 32)] = w.astype(BF16)
            else:
                g = pl.ds(pl.multiple_of(pair * 128 + j * 64, 64), 64)
                G[table, q, :, g] = w.astype(BF16)

    def emit(v, o, lo, hi):
        for g in range(lo, hi):
            w = v[(g - lo) * 64 : (g - lo) * 64 + (64 if g < 7 else 32)]
            if g < 7:
                w = w.T
                o[2 * g] = w[0:64]
                o[2 * g + 1] = w[64:128]
            else:
                w = jnp.concatenate([w, pltpu.roll(w, 64, 1)], axis=0).T
                o[14] = w[0:64]

    def halves(ref, side):
        rows = ref.shape[-2] // 2
        return ref.at[(slice(None),) * (len(ref.shape) - 2) + (pl.ds(side * rows, rows),)]

    def one_way(name, axis, part, R, side):
        me, n = spot[axis]
        m = n // 2
        to = axis + "pm"[side]
        here = part((me + m) % n)
        hop = send(halves(here, side), halves(R.at[side, 0], side), to)
        for s in range(1, m):
            yield [hop]
            here = part((me + m - s) % n if side == 0 else (me + n - m + s) % n)
            src = R.at[side, s - 1]
            if s == 1:
                halves(here, side)[...] += halves(src, side)[...]
            else:
                here[...] += src[...]
            spend(0.2)
            hop = send(here, R.at[side, s], to)
        yield [hop]
        mark("ring", name, side)

    def ring(name, axis, part, R):
        for side in range(2):
            add(0, one_way(name, axis, part, R, side))
        return [("ring", name, side) for side in range(2)]

    def total(axis, part, R):
        me, n = spot[axis]
        m = n // 2
        v = part(me)[...].astype(F32)
        if m > 1:
            return v + R[0, m - 1].astype(F32) + R[1, m - 1].astype(F32)
        rows = v.shape[-2] // 2
        r0, r1 = R[0, 0].astype(F32), R[1, 0].astype(F32)
        return v + jnp.concatenate([r0[..., :rows, :], r1[..., rows:, :]], axis=-2)

    ready_up = []

    def up_quarter(q):
        yield [("scores", r) for r in range(4)] + [cot_sib]
        for r in (0, 3, 1, 2):
            if r:
                yield [("cot", r, q)]
                yield [on[1, r, q]]
            turn(1, r, q * quarter, (q + 1) * quarter)
        mark("turned", q)

        def pairs(n, carry):
            gradient(1, q, n)
            return carry

        lax.fori_loop(0, 3, pairs, 0)
        gradient(1, q, 3)
        spend(1.8)

        def part(d):
            return G.at[1, q, d]

        yield ring(("up", q), "z", part, Rz.at[q])
        G[1, q, z] = total("z", part, Rz.at[q]).astype(BF16)
        spend(0.2)
        mark("up z", q)

    def up_rest():
        yield [("up z", q) for q in range(xs)]

        def part(d):
            return G.at[1, d, z]

        yield ring("up x", "x", part, Rx)
        emit(total("x", part, Rx), ug_o, 0, 8)
        spend(0.5)

    def down_chunk(i):
        first, lo, hi = DOWN[i]
        rows = rows_in(lo, hi)
        yield [("back", r) for r in range(4)]

        def loop(q, carry):
            gradient(0, q, lo // 2)
            return carry

        lax.fori_loop(0, xs, loop, 0)
        spend(1.8)
        Ra, Rb = down_recv[i]
        if first == "x":
            part, second, sub = (lambda d: G.at[0, d, :, rows]), "z", (lambda d: G.at[0, x, d, rows])
        else:
            part, second, sub = (lambda d: G.at[0, :, d, rows]), "x", (lambda d: G.at[0, d, z, rows])
        yield ring(("down", i), first, part, Ra)
        part(spot[first][0])[...] = total(first, part, Ra).astype(BF16)
        spend(0.2)
        yield ring(("down 2", i), second, sub, Rb)
        emit(total(second, sub, Rb), dg_o, lo, hi)
        spend(0.3)

    def forward(r):
        if r == 0:
            yield [tok_sib, pres_sib]
            for c in loads[:2]:
                c.wait()
        else:
            yield [("tok", r), ("pres", r)]
            pair = [on[0, 2, 3], on[0, 2, 1]] if r == 2 else [on[0, r, 0], on[0, r, 1]]
            yield pair + [on["pres", r]] + ([pres_near[r]] if r != 2 else [far["pres"]])
        scores(r)
        mark("scores", r)
        turn(0, r, 0, width)
        mark("turned tok", r)

    def forward_out(r):
        yield [("turned tok", r), ("loaded",)]
        if r == 2:
            yield [("sent", on[0, 2, 3]), ("sent", on[0, 2, 1])]
        partial(0, r)
        send_parts(0, r)

    def load_rest():
        yield []
        for c in loads[2:]:
            c.wait()
        mark("loaded")

    def backward(r):
        yield [("scores", r), ("loaded",)]
        if r == 0:
            yield [cot_sib]
        else:
            yield [("cot", r, q) for q in range(xs)]
            yield [on[1, r, q] for q in range(xs)]
        back(r)
        mark("back", r)

    def backward_out(r):
        yield [("back", r)] + [("turned", q) for q in range(xs)] * (r in (0, 2))
        if r == 2:
            yield [("sent", on[1, 2, q]) for q in range(xs)]
        partial(1, r)
        send_parts(1, r)

    to_sib, hop, last = {}, {}, {}

    def send_parts(a, r):
        to_sib[a, r] = send(parts_of(a, r).at[1], sibR.at[a, r], "sib")
        mark("parts", a, r)

    side_of = {3: 0, 1: 1}
    back_to = {3: "ym", 1: "yp"}

    def chip_sum(a, r):
        yield [("parts", a, r)]
        yield [to_sib[a, r]]
        parts_of(a, r).at[0][...] += sibR[a, r]
        spend(0.2)
        mark("sum", a, r)
        if r == 0:
            return
        yield [("far cot", 3, xs - 1), ("far cot", 1, xs - 1)]
        if r == 2:
            hop[a, 3] = send(A.at[a, 2, 0, TOP], R1.at[0, a], "ym")
            hop[a, 1] = send(A.at[a, 2, 0, BOTTOM], R1.at[1, a], "yp")
            mark("hop", a)
        else:
            h = other[r]
            last[a, r, 0] = send(parts_of(a, r).at[0, h], R2.at[side_of[r], a, h], back_to[r])
            mark("last", a, r, 0)

    def pass_sum(a, r):
        yield [("sum", a, r), ("hop", a), ("last", a, r, 0)]
        yield [hop[a, r]]
        h = half[r]
        parts_of(a, r).at[0, h][...] += R1[side_of[r], a]
        spend(0.1)
        last[a, r, 1] = send(parts_of(a, r).at[0, h], R2.at[side_of[r], a, h], back_to[r])
        mark("last", a, r, 1)

    def finish(a, o):
        yield [("sum", a, 0)] + [("last", a, r, i) for r in (3, 1) for i in range(2)]
        yield [last[a, r, i] for r in (3, 1) for i in range(2)]
        v = A[a, 0, 0].astype(F32) + R2[0, a].astype(F32) + R2[1, a].astype(F32)
        o[...] = v.astype(BF16)
        spend(0.4)

    for r in (3, 1):
        add(0, pass_presence(r))
    add(0, pass_far_presence())
    for r in (3, 1):
        add(0, pass_tokens(r))
    add(0, pass_far_tokens())
    for r in (3, 1):
        add(0, pass_cot(r))
    add(0, pass_far_cot())
    for r in (0, 3, 1, 2):
        add(1, forward(r))
    add(2, load_rest())
    for q in range(xs):
        add(2, up_quarter(q))
    add(6, up_rest())
    for r in (0, 3, 1, 2):
        add(3, backward(r))
    for i in range(len(DOWN)):
        add(3 if i < 2 else 5, down_chunk(i))
    for r in (0, 3, 1, 2):
        add(4, forward_out(r))
        add(4, backward_out(r))
    for a in range(2):
        for r in (2, 3, 1, 0):
            add(1, chip_sum(a, r))
        for r in (3, 1):
            add(0, pass_sum(a, r))
        add(6, finish(a, (out_o, in_o)[a]))
    run()
    for i in range(len(copies)):
        wait(i)
        wait(("sent", i))


def hand_over(*refs):
    sem = refs[12]
    moves = []
    for i in range(4):
        moves.append(pltpu.make_async_copy(refs[i], refs[8 + i], sem.at[i]))
        moves[-1].start()
    for i in range(4):
        moves[i].wait()
        moves.append(pltpu.make_async_copy(refs[8 + i], refs[4 + i], sem.at[4 + i]))
        moves[-1].start()
    for c in moves[4:]:
        c.wait()


def body(xs, zs, tokens, cotangent, down, up, ids):
    blocks, size, width = down.shape
    tile = tokens.shape[0]
    vmem = pl.BlockSpec(memory_space=pltpu.VMEM)
    scratch = [
        pltpu.VMEM((ROWS_PAD, width), BF16),
        pltpu.VMEM((ROWS_PAD, width), BF16),
        pltpu.VMEM((2, 4, 2, tile, width), BF16),
        pltpu.VMEM((2, 2, 2, tile, width), BF16),
        pltpu.VMEM((2, width, 8 * tile), BF16),
        pltpu.VMEM((2, 8 * tile, ROWS_PAD), BF16),
        pltpu.VMEM((4, 2, 8, 128), F32),
        pltpu.VMEM((2, 4, tile, width), BF16),
        pltpu.VMEM((2, 2, tile // 2, width), BF16),
        pltpu.VMEM((2, 2, tile, width), BF16),
        pltpu.VMEM((2, xs, zs, SLICE, 128), BF16),
        pltpu.VMEM((xs, 2, zs // 2, SLICE, 128), BF16),
        pltpu.VMEM((2, xs // 2, SLICE, 128), BF16),
    ]
    for first, lo, hi in DOWN:
        rows = rows_in(lo, hi).size
        if first == "x":
            scratch.append(pltpu.VMEM((2, xs // 2, zs, rows, 128), BF16))
            scratch.append(pltpu.VMEM((2, zs // 2, rows, 128), BF16))
        else:
            scratch.append(pltpu.VMEM((2, zs // 2, xs, rows, 128), BF16))
            scratch.append(pltpu.VMEM((2, xs // 2, rows, 128), BF16))
    scratch += [
        pltpu.SemaphoreType.DMA((256,)),
        pltpu.SemaphoreType.DMA((256,)),
        pltpu.SemaphoreType.DMA((4,)),
    ]
    any_spec = pl.BlockSpec(memory_space=pl.ANY)
    shapes = (
        jax.ShapeDtypeStruct((tile, width), BF16),
        jax.ShapeDtypeStruct((tile, width), BF16),
        jax.ShapeDtypeStruct((blocks, size, width // (xs * zs)), F32),
        jax.ShapeDtypeStruct((blocks, size, width // (xs * zs)), F32),
    )
    results = pl.pallas_call(
        functools.partial(kernel, xs, zs),
        out_shape=shapes,
        in_specs=[pl.BlockSpec(memory_space=pltpu.SMEM)] + [any_spec] * 4,
        out_specs=(vmem,) * 4,
        scratch_shapes=scratch,
        compiler_params=pltpu.CompilerParams(
            collective_id=0, has_side_effects=True, vmem_limit_bytes=62 * 1024 * 1024
        ),
    )(
        ids,
        tokens,
        cotangent,
        down.reshape(blocks * size, width),
        up.reshape(blocks * size, width),
    )
    return tuple(
        pl.pallas_call(
            hand_over,
            out_shape=shapes,
            in_specs=[any_spec] * 4,
            out_specs=(any_spec,) * 4,
            scratch_shapes=[pltpu.VMEM(s.shape, s.dtype) for s in shapes]
            + [pltpu.SemaphoreType.DMA((8,))],
        )(*results)
    )


def solution(mesh):
    placed = (
        P(("dp", "expert"), None),
        P(("dp", "expert"), None),
        P("expert", None, None),
        P("expert", None, None),
        P(("dp", "expert"), None),
    )
    zs = min(ZSIZE, mesh.shape["dp"])
    return jax.shard_map(
        functools.partial(body, mesh.shape["dp"] // zs, zs),
        mesh=mesh,
        in_specs=placed,
        out_specs=(
            P(("dp", "expert"), None),
            P(("dp", "expert"), None),
            P("expert", None, "dp"),
            P("expert", None, "dp"),
        ),
        check_vma=False,
    )
```

time: 704 us -> 123 us (0.17)
  waiting for transfers between devices: 477 us -> 0 us
  Pallas kernels: 0 us -> 123 us
  other arithmetic: 82.7 us -> 0 us
  local copies, waits for them, and re-layouts: 71.1 us -> 0 us
  matrix products: 46.1 us -> 0 us
  between operations: 14.2 us -> 0.8 us
  blocking collectives: 10.8 us -> 0 us
    unnamed x8 -> x0, waiting for transfers between devices: 353 us -> none
    pallas_call x0 -> x2, Pallas kernels: none -> 123 us  [the longest x1 120 us: body(): pl.pallas_call(functools.partial(kernel, xs, zs), out_shape=shapes, in_sp...]
    reduce_scatter x2 -> x0, waiting for transfers between devices: 82.6 us -> none  [the longest x1 42.3 us: body(): lax.psum_scatter(input_part.astype(jnp.bfloat16), 'expert', scatter_dimen...]
    scatter-add x2 -> x0, other arithmetic: 68.3 us -> none  [the longest x1 34.2 us: body(): empty_grads.at[flat_slots].add(up_terms.reshape(-1, expert_count, width))]
    unnamed x11 -> x0, local copies, waits for them, and re-layouts: 48.2 us -> none
    dot_general x6 -> x0, matrix products: 46.1 us -> none  [the longest x1 10.3 us: body(): jnp.einsum('gtse,gtd->gsed', hidden, all_cot, preferred_element_type=jnp....]
    all_gather x2 -> x0, waiting for transfers between devices: 41.4 us -> none  [the longest x1 29.6 us: body(): lax.all_gather(cot_tiles, 'expert', axis=0, tiled=True)]
    gather x2 -> x0, local copies, waits for them, and re-layouts: 14.2 us -> none  [the longest x1 7.11 us: body(): down_sel = jnp.take(down_vectors, safe_index, axis=0)]
  transfers between devices with their start and end apart: 6 -> 0, of which waited for: 6 -> 0; matrix products, arithmetic and copies ran while one was open for 17% -> 0% of each run, Pallas kernels for 0% -> 0%
where the time goes in v1:
time: 123 us
  Pallas kernels  123 us (100%)
    pallas_call x1, Pallas kernels, body(): pl.pallas_call(functools.partial(kernel, xs, zs), out_shape=shapes, in_sp...  120 us

profile of v1, /device:TPU:6, one launch (start us, length us, event | category | flops | bytes accessed | tf_op | source)
XLA Modules:
  0.0 123.3 jit_solution(4957259938636487491)
XLA Ops:
  0.6 120.1 %shard_map.84 = (bf16[128,2048]{1,0:T(8,128)(2,1)}, bf16[128,2048]{1,0:T(8,128)(2,1)}, f32[15,64,64]{2,1,0:T(8,128)}, f32[15,64,64]{2,1,0:T(8,128)}) custom-call(s32[1,16]{1,0:T(1,128)} %refs_0_.1, bf16[128,2048]{1,0:T(8,128)(2,1)} %refs_1_.1, bf16[128,2048]{1,0:T(8,128)(2,1)} %refs_2_.1, bf16[960,2048]{1,0:T(8,128)(2,1)} %bitcast.2, bf16[960,2048]{1,0:T(8,128)(2,1)} %bitcast.3), custom_call_target="tpu_custom_call" | custom-call | tf_op jit(solution)/shard_map/pallas_call | solution.py:589
  120.7 2.4 %shard_map.85 = (bf16[128,2048]{1,0:T(8,128)(2,1)}, bf16[128,2048]{1,0:T(8,128)(2,1)}, f32[15,64,64]{2,1,0:T(8,128)}, f32[15,64,64]{2,1,0:T(8,128)}) custom-call(bf16[128,2048]{1,0:T(8,128)(2,1)} %get-tuple-element.8.refs_0_, bf16[128,2048]{1,0:T(8,128)(2,1)} %get-tuple-element.9.refs_1_, f32[15,64,64]{2,1,0:T(8,128)} %get-tuple-element.10.refs_2_, ...), custom_call_target="tpu_custom_call" | custom-call | tf_op jit(solution)/shard_map/pallas_call | solution.py:606
